TPU v7x, 32 devices: a whole 2x2x4 slice. The times are simulated.
32 devices in a mesh: ax: 2 (over x), az: 4 (over z), rad: 4 (over y, core).
Axes of the slice: x: 2, y: 2, z: 4, core: 2. Of those that a mesh axis runs over, the one named last changes fastest.
Arguments:
- velocity: float32 [512, 64, 512], P('rad', 'az', 'ax'), may hold values from -4 to 4
- radial_courant: bfloat16 [512, 64, 512], P('rad', 'az', 'ax'), may hold values from -0.5 to 0.5
- axial_courant: bfloat16 [512, 64, 512], P('rad', 'az', 'ax'), may hold values from -0.5 to 0.5
- radial_diffusion: float32 [512], P('rad'), may hold values from 2048 to 8192
Outputs:
- advanced: float32 [512, 64, 512], P('rad', 'az', 'ax')
All inputs are finite; a program needn't handle non-finite values.
Results may differ from a plain program's by a relative error of at most 0.0009.
Values sent between devices are 32-bit elements; how exact they have to be, the bound alone decides.
A program may use at most 64 MiB of HBM per device.

v0:
```python
from functools import partial
import jax
import jax.numpy as jnp
from jax import lax
from jax.sharding import PartitionSpec as P

NR = 512
STEPS = 6
theta_rate = 0.25
axial_mixing = 0.25
azimuth_mixing = 0.25


def padded(block, sides, width, periodic):
    for axis, dim in sides:
        count = lax.axis_size(axis)
        forward = [(i, i + 1) for i in range(count - 1)]
        if periodic:
            forward.append((count - 1, 0))
        backward = [(target, source) for source, target in forward]
        low = lax.ppermute(
            lax.slice_in_dim(block, block.shape[dim] - width, None, axis=dim), axis, forward
        )
        high = lax.ppermute(lax.slice_in_dim(block, 0, width, axis=dim), axis, backward)
        block = jnp.concatenate([low, block, high], axis=dim)
    return block


def radial_terms(radial_diffusion, position):
    spacing = 1.0 / (NR + 1)
    radius = 1.0 + (position + 1.0) * spacing
    inward = radial_diffusion * (radius - 0.5 * spacing) / radius
    outward = radial_diffusion * (radius + 0.5 * spacing) / radius
    curvature = radial_diffusion * spacing * spacing / (radius * radius)
    return (radius, inward, outward, curvature)


def right_side(
    state_field,
    radial_lower,
    radial_upper,
    axial_minus_two,
    axial_minus_one,
    axial_plus_one,
    axial_plus_two,
    azimuth_minus_two,
    azimuth_minus_one,
    azimuth_plus_one,
    azimuth_plus_two,
    radial_courant,
    axial_courant,
    radius,
    inward,
    outward,
    curvature,
):
    radius_col = radius[:, None, None]
    spread = (
        outward[:, None, None] * (radial_upper - state_field)
        - inward[:, None, None] * (state_field - radial_lower)
        - curvature[:, None, None] * state_field
    )
    radial_slope = 0.5 * (radial_upper - radial_lower)
    axial_slope = (
        8.0 * (axial_plus_one - axial_minus_one) - (axial_plus_two - axial_minus_two)
    ) / 12.0
    axial_curve = (
        16.0 * (axial_plus_one + axial_minus_one)
        - (axial_plus_two + axial_minus_two)
        - 30.0 * state_field
    ) / 12.0
    azimuth_slope = (
        8.0 * (azimuth_plus_one - azimuth_minus_one) - (azimuth_plus_two - azimuth_minus_two)
    ) / 12.0
    azimuth_curve = (
        16.0 * (azimuth_plus_one + azimuth_minus_one)
        - (azimuth_plus_two + azimuth_minus_two)
        - 30.0 * state_field
    ) / 12.0
    transport = (
        radial_courant * radial_slope
        + axial_courant * axial_slope
        + theta_rate * state_field * azimuth_slope / radius_col
    )
    mixing = axial_mixing * axial_curve + azimuth_mixing * azimuth_curve / (radius_col * radius_col)
    return state_field + spread - transport + mixing


def neighbours(state_field):
    slab_rows, theta_cells, axial_cells = state_field.shape
    radial_ext = padded(state_field, (("rad", 0),), 1, False)
    radial_lower = radial_ext[:-2]
    radial_upper = radial_ext[2:]
    azimuth_ext = padded(state_field, (("az", 1),), 2, True)
    axial_ext = padded(state_field, (("ax", 2),), 2, False)
    return (
        radial_lower,
        radial_upper,
        axial_ext[:, :, 0:axial_cells],
        axial_ext[:, :, 1 : axial_cells + 1],
        axial_ext[:, :, 3 : axial_cells + 3],
        axial_ext[:, :, 4 : axial_cells + 4],
        azimuth_ext[:, 0:theta_cells],
        azimuth_ext[:, 1 : theta_cells + 1],
        azimuth_ext[:, 3 : theta_cells + 3],
        azimuth_ext[:, 4 : theta_cells + 4],
    )


def join_slabs(earlier, later_seg):
    head_left, tail_left, tips_left = earlier
    head_right, tail_right, tips_right = later_seg
    divisor = 1.0 - tips_left[3] * tips_right[0]
    mid_value = (tail_left - tips_left[3] * head_right) / divisor
    mid_left = tips_left[2] / divisor
    mid_right = -tips_left[3] * tips_right[1] / divisor
    next_value = head_right - tips_right[0] * mid_value
    next_left = -tips_right[0] * mid_left
    next_right = tips_right[1] - tips_right[0] * mid_right
    new_head = head_left - tips_left[1] * next_value
    new_tail = tail_right - tips_right[2] * mid_value
    new_tips = jnp.stack(
        [
            tips_left[0] - tips_left[1] * next_left,
            -tips_left[1] * next_right,
            -tips_right[2] * mid_left,
            tips_right[3] - tips_right[2] * mid_right,
        ]
    )
    return (new_head, new_tail, new_tips)


def choose(keep_new, fresh_value, stale_value):
    return jnp.where(keep_new, fresh_value, stale_value)


def settle(prefix, own_slab, suffix):
    combined = join_slabs(own_slab, suffix)
    pre_first, pre_last, pre_tips = prefix
    own_first, own_last, own_tips = own_slab
    suf_first, suf_last, suf_tips = suffix
    lower_value = (pre_last - pre_tips[3] * combined[0]) / (1.0 - pre_tips[3] * combined[2][0])
    upper_value = (suf_first - suf_tips[0] * (own_last - own_tips[2] * lower_value)) / (
        1.0 - suf_tips[0] * own_tips[3]
    )
    return (lower_value, upper_value)


def interface(first_row, last_row, spike_tips, every_tips):
    own_slab = (first_row, last_row, spike_tips)
    identity = (
        jnp.zeros_like(first_row),
        jnp.zeros_like(last_row),
        jnp.array([0.0, -1.0, -1.0, 0.0], jnp.float32),
    )
    every_first, every_last = (
        lax.all_gather(first_row[None], "rad", axis=0, tiled=True),
        lax.all_gather(last_row[None], "rad", axis=0, tiled=True),
    )
    position = lax.axis_index("rad")
    slab_count = lax.axis_size("rad")
    prefix = identity
    for index_k in range(slab_count):
        member = (every_first[index_k], every_last[index_k], every_tips[index_k])
        joined = join_slabs(prefix, member)
        prefix = jax.tree.map(partial(choose, index_k < position), joined, prefix)
    suffix = identity
    for index_k in range(slab_count - 1, -1, -1):
        member = (every_first[index_k], every_last[index_k], every_tips[index_k])
        joined = join_slabs(member, suffix)
        suffix = jax.tree.map(partial(choose, index_k > position), joined, suffix)
    return settle(prefix, own_slab, suffix)


def local(velocity, radial_courant, axial_courant, radial_diffusion):
    slab_rows = velocity.shape[0]
    start_row = (lax.axis_index("rad") * slab_rows).astype(jnp.float32)
    position = start_row + jnp.arange(slab_rows).astype(jnp.float32)
    radius, inward, outward, curvature = radial_terms(radial_diffusion, position)
    zero_one = jnp.zeros((1,), jnp.float32)
    lower_diag = jnp.concatenate([zero_one, -inward[1:]])
    upper_diag = jnp.concatenate([-outward[:-1], zero_one])
    main_diag = 1.0 + inward + outward + curvature
    inverse = lax.linalg.tridiagonal_solve(
        lower_diag, main_diag, upper_diag, jnp.eye(slab_rows, dtype=jnp.float32)
    )
    left_spike = -inward[0] * inverse[:, 0]
    right_spike = -outward[-1] * inverse[:, -1]
    spike_tips = jnp.stack([left_spike[0], right_spike[0], left_spike[-1], right_spike[-1]])
    every_tips = lax.all_gather(spike_tips[None], "rad", axis=0, tiled=True)
    state_field = velocity
    for turn_index in range(STEPS):
        right_hand = right_side(
            state_field,
            *neighbours(state_field),
            radial_courant,
            axial_courant,
            radius,
            inward,
            outward,
            curvature
        )
        flat_rhs = right_hand.reshape(slab_rows, -1)
        slab_solution = jnp.dot(
            inverse, flat_rhs, precision=lax.Precision.HIGHEST, preferred_element_type=jnp.float32
        )
        lower_value, upper_value = interface(
            slab_solution[0], slab_solution[-1], spike_tips, every_tips
        )
        solved = (
            slab_solution
            - left_spike[:, None] * lower_value[None, :]
            - right_spike[:, None] * upper_value[None, :]
        )
        state_field = solved.reshape(state_field.shape)
    return state_field


def solution(mesh):
    return jax.shard_map(
        local,
        mesh=mesh,
        in_specs=(P("rad", "az", "ax"), P("rad", "az", "ax"), P("rad", "az", "ax"), P("rad")),
        out_specs=P("rad", "az", "ax"),
        check_vma=False,
    )
```

profile of v0, /device:TPU:0, one launch (start us, length us, event | category | flops | bytes accessed | tf_op | source)
XLA Modules:
  0.0 981.2 jit_solution(10601417094346248530)
XLA Ops:
  16.5 5.7 collective-permute-start.3
  26.0 253.8 %while.32 = (s32[]{:T(128)}, f32[]{:T(128)}, f32[128]{0:T(128)S(1)}, f32[3,32]{1,0:T(4,128)S(1)}, f32[3,32,128]{2,1,0:T(8,128)S(1)}, /*index=5*/f32[3,32]{1,0:T(...) while((s32[]{:T(128)}, f32[]{:T(128)}, ...), condition=%wide.region_1.2_spmd, body=%wide.region_0.1_spmd.sunk | while | flops 12417 | bytes 104185 | solution.py:184
  90.2 20.2 %fusion.565 = (f32[128]{0:T(128)S(1)}, f32[128]{0:T(128)S(1)}, f32[128]{0:T(128)S(1)}, f32[128]{0:T(128)S(1)}, f32[128]{0:T(128)S(1)}, /*index=5*/f32[128]{0:T(1...) fusion(f32[3,32,128]{2,1,0:T(8,128)S(1)} %get-tuple-element.125, ...), kind=kLoop, calls=%fused_computation.41.clone.1 | loop fusion | flops 12288 | bytes 33664 | tf_op jit(solution)/shard_map/while/body/eval_jaxpr/div | solution.py:184
  174.8 20.2 %fusion.565 = (f32[128]{0:T(128)S(1)}, f32[128]{0:T(128)S(1)}, f32[128]{0:T(128)S(1)}, f32[128]{0:T(128)S(1)}, f32[128]{0:T(128)S(1)}, /*index=5*/f32[128]{0:T(1...) fusion(f32[3,32,128]{2,1,0:T(8,128)S(1)} %get-tuple-element.125, ...), kind=kLoop, calls=%fused_computation.41.clone.1 | loop fusion | flops 12288 | bytes 33664 | tf_op jit(solution)/shard_map/while/body/eval_jaxpr/div | solution.py:184
  259.4 20.2 %fusion.565 = (f32[128]{0:T(128)S(1)}, f32[128]{0:T(128)S(1)}, f32[128]{0:T(128)S(1)}, f32[128]{0:T(128)S(1)}, f32[128]{0:T(128)S(1)}, /*index=5*/f32[128]{0:T(1...) fusion(f32[3,32,128]{2,1,0:T(8,128)S(1)} %get-tuple-element.125, ...), kind=kLoop, calls=%fused_computation.41.clone.1 | loop fusion | flops 12288 | bytes 33664 | tf_op jit(solution)/shard_map/while/body/eval_jaxpr/div | solution.py:184
  342.2 19.2 %fusion.330 = (f32[128]{0:T(128)S(1)}, f32[128]{0:T(128)S(1)}, f32[128]{0:T(128)S(1)}, f32[128]{0:T(128)S(1)}, f32[128]{0:T(128)S(1)}, /*index=5*/f32[128]{0:T(1...) fusion(f32[128,128]{1,0:T(8,128)S(1)} %fusion.256, ...), kind=kLoop, calls=%fused_computation.662 | loop fusion | flops 11904 | bytes 32504 | tf_op jit(solution)/shard_map/eval_jaxpr/div | solution.py:184
  361.8 65.2 %while.33 = (s32[]{:T(128)}, f32[128]{0:T(128)S(1)}, f32[3,32,128]{2,1,0:T(8,128)S(1)}, f32[3,32,128]{2,1,0:T(8,128)S(1)}, f32[3,32]{1,0:T(4,128)S(1)}, /*index=...) while((s32[]{:T(128)}, f32[128]{0:T(128)S(1)}, ...), condition=%wide.region_3.4_spmd, body=%wide.region_2.3_spmd.sunk | while | flops 8226 | bytes 101341 | solution.py:184
  363.3 20.2 %fusion.568 = (f32[128]{0:T(128)S(1)}, f32[128]{0:T(128)S(1)}, f32[128]{0:T(128)S(1)}, f32[128]{0:T(128)S(1)}, f32[128]{0:T(128)S(1)}, /*index=5*/f32[128]{0:T(1...) fusion(f32[3,32,128]{2,1,0:T(8,128)S(1)} %get-tuple-element.136, ...), kind=kLoop, calls=%fused_computation.169.clone.1 | loop fusion | flops 8192 | bytes 33536 | tf_op jit(solution)/shard_map/while/body/eval_jaxpr/sub | solution.py:184
  385.0 20.2 %fusion.568 = (f32[128]{0:T(128)S(1)}, f32[128]{0:T(128)S(1)}, f32[128]{0:T(128)S(1)}, f32[128]{0:T(128)S(1)}, f32[128]{0:T(128)S(1)}, /*index=5*/f32[128]{0:T(1...) fusion(f32[3,32,128]{2,1,0:T(8,128)S(1)} %get-tuple-element.136, ...), kind=kLoop, calls=%fused_computation.169.clone.1 | loop fusion | flops 8192 | bytes 33536 | tf_op jit(solution)/shard_map/while/body/eval_jaxpr/sub | solution.py:184
  406.8 20.2 %fusion.568 = (f32[128]{0:T(128)S(1)}, f32[128]{0:T(128)S(1)}, f32[128]{0:T(128)S(1)}, f32[128]{0:T(128)S(1)}, f32[128]{0:T(128)S(1)}, /*index=5*/f32[128]{0:T(1...) fusion(f32[3,32,128]{2,1,0:T(8,128)S(1)} %get-tuple-element.136, ...), kind=kLoop, calls=%fused_computation.169.clone.1 | loop fusion | flops 8192 | bytes 33536 | tf_op jit(solution)/shard_map/while/body/eval_jaxpr/sub | solution.py:184
  436.2 3.4 fusion.375
  439.6 3.3 fusion.374
  442.9 3.3 fusion.373
  494.3 6.0 all-reduce
  580.3 14.9 %fusion.181 = f32[128,16,256]{2,1,0:T(8,128)S(1)} fusion(bf16[128,16,256]{2,1,0:T(8,128)(2,1)S(1)} %copy-done, bf16[128,16,256]{2,1,0:T(8,128)(2,1)S(1)} %copy-done.1, f32[128,16,256]{2,1,0:T(8,128)} %param.14, f32[1,16,256]{2,1,0:T(8,128)} %collective-permute-done.1, f32[1,16,256]{2,1,0:T(8,128)S(1)} %collective-permute-done, ...), kind=kLoop, calls=%fused_computation.299 | loop fusion | flops 28311552 | bytes 10816000 | tf_op jit(solution)/shard_map/add | solution.py:86
  598.9 5.9 all-gather.2
  604.8 5.2 all-gather.1
  610.0 13.5 %subtract_divide_fusion.5 = (f32[1,4096]{1,0:T(1,128)S(1)}, f32[1,4096]{1,0:T(1,128)S(1)}) fusion(f32[]{:T(128)} %bitcast.672, f32[]{:T(128)S(6)} %sub.2725, f32[]{:T(128)S(1)} %bitcast.2392, f32[128,4096]{1,0:T(8,128)S(1)} %fusion.531, f32[]{:T(128)S(6)} %sub.2730, f32[]{:T(128)} %bitcast.670, f32[]{:T(128)} %bitcast.640, f32[]{:T(128)} %bitcast.639, ...), kind=kLoop, calls=%fused_computation.547 | loop fusion | flops 286720 | bytes 196748 | tf_op jit(solution)/shard_map/div | solution.py:143
  627.9 3.8 collective-permute-start.10
  639.0 5.1 collective-permute-start.9
  654.5 9.4 fusion.185
  667.6 7.8 all-gather.4
  675.3 5.5 all-gather.3
  680.9 13.5 %subtract_divide_fusion.4 = (f32[1,4096]{1,0:T(1,128)S(1)}, f32[1,4096]{1,0:T(1,128)S(1)}) fusion(f32[]{:T(128)} %bitcast.672, f32[]{:T(128)S(6)} %sub.2725, f32[]{:T(128)S(1)} %bitcast.2393, f32[128,4096]{1,0:T(8,128)S(1)} %fusion.532, f32[]{:T(128)S(6)} %sub.2730, f32[]{:T(128)} %bitcast.670, f32[]{:T(128)} %bitcast.640, f32[]{:T(128)} %bitcast.639, ...), kind=kLoop, calls=%fused_computation.546 | loop fusion | flops 286720 | bytes 196748 | tf_op jit(solution)/shard_map/div | solution.py:143
  698.7 3.8 collective-permute-start.16
  709.8 5.1 collective-permute-start.15
  725.3 9.4 fusion.189
  738.4 7.9 all-gather.6
  746.3 5.5 all-gather.5
  751.9 13.5 %subtract_divide_fusion.3 = (f32[1,4096]{1,0:T(1,128)S(1)}, f32[1,4096]{1,0:T(1,128)S(1)}) fusion(f32[]{:T(128)} %bitcast.672, f32[]{:T(128)S(6)} %sub.2725, f32[]{:T(128)S(1)} %bitcast.2394, f32[128,4096]{1,0:T(8,128)S(1)} %fusion.533, f32[]{:T(128)S(6)} %sub.2730, f32[]{:T(128)} %bitcast.670, f32[]{:T(128)} %bitcast.640, f32[]{:T(128)} %bitcast.639, ...), kind=kLoop, calls=%fused_computation.545 | loop fusion | flops 286720 | bytes 196748 | tf_op jit(solution)/shard_map/div | solution.py:143
  769.7 3.8 collective-permute-start.22
  780.8 5.1 collective-permute-start.21
  796.6 9.4 fusion.193
  809.6 7.9 all-gather.8
  817.6 5.5 all-gather.7
  823.1 13.5 %subtract_divide_fusion.2 = (f32[1,4096]{1,0:T(1,128)S(1)}, f32[1,4096]{1,0:T(1,128)S(1)}) fusion(f32[]{:T(128)} %bitcast.672, f32[]{:T(128)S(6)} %sub.2725, f32[]{:T(128)S(1)} %bitcast.2395, f32[128,4096]{1,0:T(8,128)S(1)} %fusion.534, f32[]{:T(128)S(6)} %sub.2730, f32[]{:T(128)} %bitcast.670, f32[]{:T(128)} %bitcast.640, f32[]{:T(128)} %bitcast.639, ...), kind=kLoop, calls=%fused_computation.544 | loop fusion | flops 286720 | bytes 196748 | tf_op jit(solution)/shard_map/div | solution.py:143
  840.9 3.8 collective-permute-start.28
  852.0 5.1 collective-permute-start.27
  867.5 9.4 fusion.197
  880.6 7.9 all-gather.10
  888.5 5.5 all-gather.9
  894.1 13.5 %subtract_divide_fusion.1 = (f32[1,4096]{1,0:T(1,128)S(1)}, f32[1,4096]{1,0:T(1,128)S(1)}) fusion(f32[]{:T(128)} %bitcast.672, f32[]{:T(128)S(6)} %sub.2725, f32[]{:T(128)S(1)} %bitcast.2396, f32[128,4096]{1,0:T(8,128)S(1)} %fusion.535, f32[]{:T(128)S(6)} %sub.2730, f32[]{:T(128)} %bitcast.670, f32[]{:T(128)} %bitcast.640, f32[]{:T(128)} %bitcast.639, ...), kind=kLoop, calls=%fused_computation.543 | loop fusion | flops 286720 | bytes 196748 | tf_op jit(solution)/shard_map/div | solution.py:143
  911.9 3.8 collective-permute-start.34
  923.0 5.1 collective-permute-start.33
  938.6 9.4 fusion.201
  951.6 7.9 all-gather.12
  959.6 5.5 all-gather.11
  965.1 13.5 %subtract_divide_fusion = (f32[1,4096]{1,0:T(1,128)S(1)}, f32[1,4096]{1,0:T(1,128)S(1)}) fusion(f32[]{:T(128)} %bitcast.672, f32[]{:T(128)S(6)} %sub.2725, f32[]{:T(128)S(1)} %bitcast.2397, f32[128,4096]{1,0:T(8,128)S(1)} %fusion.536, f32[]{:T(128)S(6)} %sub.2730, f32[]{:T(128)} %bitcast.670, f32[]{:T(128)} %bitcast.640, f32[]{:T(128)} %bitcast.639, ...), kind=kLoop, calls=%fused_computation.542 | loop fusion | flops 286720 | bytes 196748 | tf_op jit(solution)/shard_map/div | solution.py:143
  (333 shorter events, 247.9 us)
Async XLA Ops:
  1.3 579.0 %collective-permute-start.1 = (f32[1,16,256]{2,1,0:T(8,128)}, f32[1,16,256]{2,1,0:T(8,128)}, u32[]{:S(2)}, u32[]{:S(2)}) collective-permute-start(f32[1,16,256]{2,1,0:T(8,128)} %get-tuple-element.511), channel_id=1, source_target_pairs={{0,1},{1,2},{2,3},{4,5},{5,6},{6,7},{8,9},{9,10},{10,11},{12,13},{... | collective-permute-start | bytes 49160 | tf_op jit(solution)/shard_map/ppermute | solution.py:21
  6.8 573.5 %collective-permute-start.5 = (f32[128,2,256]{2,1,0:T(2,128)}, f32[128,2,256]{2,1,0:T(2,128)S(1)}, u32[]{:S(2)}, u32[]{:S(2)}) collective-permute-start(f32[128,2,256]{2,1,0:T(2,128)} %get-tuple-element.509), channel_id=1, source_target_pairs={{0,4},{4,8},{8,12},{12,0},{1,5},{5,9},{9,13},{13,1},{2,6},{6,10},{... | collective-permute-start | bytes 786440 | tf_op jit(solution)/shard_map/ppermute | solution.py:21
  9.2 569.3 %collective-permute-start.4 = (f32[128,2,256]{2,1,0:T(2,128)}, f32[128,2,256]{2,1,0:T(2,128)}, u32[]{:S(2)}, u32[]{:S(2)}) collective-permute-start(f32[128,2,256]{2,1,0:T(2,128)} %get-tuple-element.508), channel_id=1, source_target_pairs={{4,0},{8,4},{12,8},{0,12},{5,1},{9,5},{13,9},{1,13},{6,2},{10,6},{... | collective-permute-start | bytes 786440 | tf_op jit(solution)/shard_map/ppermute | solution.py:24
  13.1 9.2 copy-start.10
  14.2 559.2 %collective-permute-start.2 = (f32[128,16,2]{0,1,2:T(8,128)}, f32[128,16,2]{0,1,2:T(8,128)}, u32[]{:S(2)}, u32[]{:S(2)}) collective-permute-start(f32[128,16,2]{0,1,2:T(8,128)} %copy.101), channel_id=1, source_target_pairs={{16,0},{17,1},{18,2},{19,3},{20,4},{21,5},{22,6},{23,7},{24,8},{25... | collective-permute-start | bytes 49160 | tf_op jit(solution)/shard_map/ppermute | solution.py:24
  16.5 559.9 %collective-permute-start.3 = (f32[128,16,2]{0,1,2:T(8,128)}, f32[128,16,2]{0,1,2:T(8,128)}, u32[]{:S(2)}, u32[]{:S(2)}) collective-permute-start(f32[128,16,2]{0,1,2:T(8,128)} %copy.102), channel_id=1, source_target_pairs={{0,16},{1,17},{2,18},{3,19},{4,20},{5,21},{6,22},{7,23},{8,24},{9,... | collective-permute-start | bytes 49160 | tf_op jit(solution)/shard_map/ppermute | solution.py:21
  279.8 147.2 %copy-start.8 = (f32[3,32,128]{2,1,0:T(8,128)}, f32[3,32,128]{2,1,0:T(8,128)S(1)}, u32[]{:S(2)}) copy-start(f32[3,32,128]{2,1,0:T(8,128)S(1)} %get-tuple-element.159) | copy-start | bytes 147460
  471.3 96.4 %copy-start.2 = (f32[128,16,256]{2,1,0:T(8,128)S(1)}, f32[128,16,256]{2,1,0:T(8,128)}, u32[]{:S(2)}) copy-start(f32[128,16,256]{2,1,0:T(8,128)} %param.14) | copy-start | bytes 6291460
  567.8 5.6 copy-start.9
  569.3 11.0 %copy-start = (bf16[128,16,256]{2,1,0:T(8,128)(2,1)S(1)}, bf16[128,16,256]{2,1,0:T(8,128)(2,1)}, u32[]{:S(2)}) copy-start(bf16[128,16,256]{2,1,0:T(8,128)(2,1)} %param.15) | copy-start | bytes 3145732
  569.3 11.0 %copy-start.1 = (bf16[128,16,256]{2,1,0:T(8,128)(2,1)S(1)}, bf16[128,16,256]{2,1,0:T(8,128)(2,1)}, u32[]{:S(2)}) copy-start(bf16[128,16,256]{2,1,0:T(8,128)(2,1)} %param.16) | copy-start | bytes 3145732
  573.4 6.9 collective-permute-start
  623.9 1.3 copy-start.3
  627.9 26.6 %collective-permute-start.11 = (f32[128,2,256]{2,1,0:T(2,128)}, f32[128,2,256]{2,1,0:T(2,128)S(1)}, u32[]{:S(2)}, u32[]{:S(2)}) collective-permute-start(f32[128,2,256]{2,1,0:T(2,128)} %get-tuple-element.503), channel_id=1, source_target_pairs={{0,4},{4,8},{8,12},{12,0},{1,5},{5,9},{9,13},{13,1},{2,6},{6,10},{... | collective-permute-start | bytes 786440 | tf_op jit(solution)/shard_map/ppermute | solution.py:21
  627.9 24.8 %collective-permute-start.10 = (f32[128,2,256]{2,1,0:T(2,128)}, f32[128,2,256]{2,1,0:T(2,128)}, u32[]{:S(2)}, u32[]{:S(2)}) collective-permute-start(f32[128,2,256]{2,1,0:T(2,128)} %get-tuple-element.502), channel_id=1, source_target_pairs={{4,0},{8,4},{12,8},{0,12},{5,1},{9,5},{13,9},{1,13},{6,2},{10,6},{... | collective-permute-start | bytes 786440 | tf_op jit(solution)/shard_map/ppermute | solution.py:24
  635.4 12.2 %collective-permute-start.8 = (f32[128,16,2]{0,1,2:T(8,128)}, f32[128,16,2]{0,1,2:T(8,128)S(1)}, u32[]{:S(2)}, u32[]{:S(2)}) collective-permute-start(f32[128,16,2]{0,1,2:T(8,128)} %copy.103), channel_id=1, source_target_pairs={{16,0},{17,1},{18,2},{19,3},{20,4},{21,5},{22,6},{23,7},{24,8},{25... | collective-permute-start | bytes 49160 | tf_op jit(solution)/shard_map/ppermute | solution.py:24
  639.0 11.6 %collective-permute-start.9 = (f32[128,16,2]{0,1,2:T(8,128)}, f32[128,16,2]{0,1,2:T(8,128)}, u32[]{:S(2)}, u32[]{:S(2)}) collective-permute-start(f32[128,16,2]{0,1,2:T(8,128)} %copy.104), channel_id=1, source_target_pairs={{0,16},{1,17},{2,18},{3,19},{4,20},{5,21},{6,22},{7,23},{8,24},{9,... | collective-permute-start | bytes 49160 | tf_op jit(solution)/shard_map/ppermute | solution.py:21
  645.7 8.7 collective-permute-start.7
  647.6 6.8 collective-permute-start.6
  694.7 1.3 copy-start.4
  698.7 26.7 %collective-permute-start.17 = (f32[128,2,256]{2,1,0:T(2,128)}, f32[128,2,256]{2,1,0:T(2,128)S(1)}, u32[]{:S(2)}, u32[]{:S(2)}) collective-permute-start(f32[128,2,256]{2,1,0:T(2,128)} %get-tuple-element.497), channel_id=1, source_target_pairs={{0,4},{4,8},{8,12},{12,0},{1,5},{5,9},{9,13},{13,1},{2,6},{6,10},{... | collective-permute-start | bytes 786440 | tf_op jit(solution)/shard_map/ppermute | solution.py:21
  698.7 24.9 %collective-permute-start.16 = (f32[128,2,256]{2,1,0:T(2,128)}, f32[128,2,256]{2,1,0:T(2,128)}, u32[]{:S(2)}, u32[]{:S(2)}) collective-permute-start(f32[128,2,256]{2,1,0:T(2,128)} %get-tuple-element.496), channel_id=1, source_target_pairs={{4,0},{8,4},{12,8},{0,12},{5,1},{9,5},{13,9},{1,13},{6,2},{10,6},{... | collective-permute-start | bytes 786440 | tf_op jit(solution)/shard_map/ppermute | solution.py:24
  706.3 12.2 %collective-permute-start.14 = (f32[128,16,2]{0,1,2:T(8,128)}, f32[128,16,2]{0,1,2:T(8,128)S(1)}, u32[]{:S(2)}, u32[]{:S(2)}) collective-permute-start(f32[128,16,2]{0,1,2:T(8,128)} %copy.105), channel_id=1, source_target_pairs={{16,0},{17,1},{18,2},{19,3},{20,4},{21,5},{22,6},{23,7},{24,8},{25... | collective-permute-start | bytes 49160 | tf_op jit(solution)/shard_map/ppermute | solution.py:24
  709.8 11.6 %collective-permute-start.15 = (f32[128,16,2]{0,1,2:T(8,128)}, f32[128,16,2]{0,1,2:T(8,128)}, u32[]{:S(2)}, u32[]{:S(2)}) collective-permute-start(f32[128,16,2]{0,1,2:T(8,128)} %copy.106), channel_id=1, source_target_pairs={{0,16},{1,17},{2,18},{3,19},{4,20},{5,21},{6,22},{7,23},{8,24},{9,... | collective-permute-start | bytes 49160 | tf_op jit(solution)/shard_map/ppermute | solution.py:21
  716.6 8.8 collective-permute-start.13
  718.5 6.9 collective-permute-start.12
  765.7 1.3 copy-start.5
  769.7 26.8 %collective-permute-start.23 = (f32[128,2,256]{2,1,0:T(2,128)}, f32[128,2,256]{2,1,0:T(2,128)S(1)}, u32[]{:S(2)}, u32[]{:S(2)}) collective-permute-start(f32[128,2,256]{2,1,0:T(2,128)} %get-tuple-element.491), channel_id=1, source_target_pairs={{0,4},{4,8},{8,12},{12,0},{1,5},{5,9},{9,13},{13,1},{2,6},{6,10},{... | collective-permute-start | bytes 786440 | tf_op jit(solution)/shard_map/ppermute | solution.py:21
  769.7 25.0 %collective-permute-start.22 = (f32[128,2,256]{2,1,0:T(2,128)}, f32[128,2,256]{2,1,0:T(2,128)}, u32[]{:S(2)}, u32[]{:S(2)}) collective-permute-start(f32[128,2,256]{2,1,0:T(2,128)} %get-tuple-element.490), channel_id=1, source_target_pairs={{4,0},{8,4},{12,8},{0,12},{5,1},{9,5},{13,9},{1,13},{6,2},{10,6},{... | collective-permute-start | bytes 786440 | tf_op jit(solution)/shard_map/ppermute | solution.py:24
  777.3 12.2 %collective-permute-start.20 = (f32[128,16,2]{0,1,2:T(8,128)}, f32[128,16,2]{0,1,2:T(8,128)S(1)}, u32[]{:S(2)}, u32[]{:S(2)}) collective-permute-start(f32[128,16,2]{0,1,2:T(8,128)} %copy.107), channel_id=1, source_target_pairs={{16,0},{17,1},{18,2},{19,3},{20,4},{21,5},{22,6},{23,7},{24,8},{25... | collective-permute-start | bytes 49160 | tf_op jit(solution)/shard_map/ppermute | solution.py:24
  780.8 11.8 %collective-permute-start.21 = (f32[128,16,2]{0,1,2:T(8,128)}, f32[128,16,2]{0,1,2:T(8,128)}, u32[]{:S(2)}, u32[]{:S(2)}) collective-permute-start(f32[128,16,2]{0,1,2:T(8,128)} %copy.108), channel_id=1, source_target_pairs={{0,16},{1,17},{2,18},{3,19},{4,20},{5,21},{6,22},{7,23},{8,24},{9,... | collective-permute-start | bytes 49160 | tf_op jit(solution)/shard_map/ppermute | solution.py:21
  787.6 9.0 collective-permute-start.19
  789.5 7.1 collective-permute-start.18
  836.9 1.3 copy-start.6
  840.9 26.6 %collective-permute-start.29 = (f32[128,2,256]{2,1,0:T(2,128)}, f32[128,2,256]{2,1,0:T(2,128)S(1)}, u32[]{:S(2)}, u32[]{:S(2)}) collective-permute-start(f32[128,2,256]{2,1,0:T(2,128)} %get-tuple-element.485), channel_id=1, source_target_pairs={{0,4},{4,8},{8,12},{12,0},{1,5},{5,9},{9,13},{13,1},{2,6},{6,10},{... | collective-permute-start | bytes 786440 | tf_op jit(solution)/shard_map/ppermute | solution.py:21
  840.9 24.8 %collective-permute-start.28 = (f32[128,2,256]{2,1,0:T(2,128)}, f32[128,2,256]{2,1,0:T(2,128)}, u32[]{:S(2)}, u32[]{:S(2)}) collective-permute-start(f32[128,2,256]{2,1,0:T(2,128)} %get-tuple-element.484), channel_id=1, source_target_pairs={{4,0},{8,4},{12,8},{0,12},{5,1},{9,5},{13,9},{1,13},{6,2},{10,6},{... | collective-permute-start | bytes 786440 | tf_op jit(solution)/shard_map/ppermute | solution.py:24
  848.5 12.2 %collective-permute-start.26 = (f32[128,16,2]{0,1,2:T(8,128)}, f32[128,16,2]{0,1,2:T(8,128)S(1)}, u32[]{:S(2)}, u32[]{:S(2)}) collective-permute-start(f32[128,16,2]{0,1,2:T(8,128)} %copy.109), channel_id=1, source_target_pairs={{16,0},{17,1},{18,2},{19,3},{20,4},{21,5},{22,6},{23,7},{24,8},{25... | collective-permute-start | bytes 49160 | tf_op jit(solution)/shard_map/ppermute | solution.py:24
  852.0 11.6 %collective-permute-start.27 = (f32[128,16,2]{0,1,2:T(8,128)}, f32[128,16,2]{0,1,2:T(8,128)}, u32[]{:S(2)}, u32[]{:S(2)}) collective-permute-start(f32[128,16,2]{0,1,2:T(8,128)} %copy.110), channel_id=1, source_target_pairs={{0,16},{1,17},{2,18},{3,19},{4,20},{5,21},{6,22},{7,23},{8,24},{9,... | collective-permute-start | bytes 49160 | tf_op jit(solution)/shard_map/ppermute | solution.py:21
  858.8 8.7 collective-permute-start.25
  860.7 6.8 collective-permute-start.24
  907.9 1.3 copy-start.7
  911.9 26.7 %collective-permute-start.35 = (f32[128,2,256]{2,1,0:T(2,128)}, f32[128,2,256]{2,1,0:T(2,128)S(1)}, u32[]{:S(2)}, u32[]{:S(2)}) collective-permute-start(f32[128,2,256]{2,1,0:T(2,128)} %get-tuple-element.479), channel_id=1, source_target_pairs={{0,4},{4,8},{8,12},{12,0},{1,5},{5,9},{9,13},{13,1},{2,6},{6,10},{... | collective-permute-start | bytes 786440 | tf_op jit(solution)/shard_map/ppermute | solution.py:21
  911.9 24.9 %collective-permute-start.34 = (f32[128,2,256]{2,1,0:T(2,128)}, f32[128,2,256]{2,1,0:T(2,128)}, u32[]{:S(2)}, u32[]{:S(2)}) collective-permute-start(f32[128,2,256]{2,1,0:T(2,128)} %get-tuple-element.478), channel_id=1, source_target_pairs={{4,0},{8,4},{12,8},{0,12},{5,1},{9,5},{13,9},{1,13},{6,2},{10,6},{... | collective-permute-start | bytes 786440 | tf_op jit(solution)/shard_map/ppermute | solution.py:24
  919.5 12.2 %collective-permute-start.32 = (f32[128,16,2]{0,1,2:T(8,128)}, f32[128,16,2]{0,1,2:T(8,128)S(1)}, u32[]{:S(2)}, u32[]{:S(2)}) collective-permute-start(f32[128,16,2]{0,1,2:T(8,128)} %copy.111), channel_id=1, source_target_pairs={{16,0},{17,1},{18,2},{19,3},{20,4},{21,5},{22,6},{23,7},{24,8},{25... | collective-permute-start | bytes 49160 | tf_op jit(solution)/shard_map/ppermute | solution.py:24
  923.0 11.6 %collective-permute-start.33 = (f32[128,16,2]{0,1,2:T(8,128)}, f32[128,16,2]{0,1,2:T(8,128)}, u32[]{:S(2)}, u32[]{:S(2)}) collective-permute-start(f32[128,16,2]{0,1,2:T(8,128)} %copy.112), channel_id=1, source_target_pairs={{0,16},{1,17},{2,18},{3,19},{4,20},{5,21},{6,22},{7,23},{8,24},{9,... | collective-permute-start | bytes 49160 | tf_op jit(solution)/shard_map/ppermute | solution.py:21
  929.8 8.8 collective-permute-start.31
  931.7 6.9 collective-permute-start.30
where the time goes:
time: 998 us; the launch traced here: 981 us
  other arithmetic  333 us (33%)
  loops' own time  180 us (18%)
  local copies, waits for them, and re-layouts  166 us (17%)
  between operations  126 us (13%)
  blocking collectives  84.3 us (8%)
  starting transfers between devices  81.3 us (8%)
  matrix products  11.7 us (1%)
    another operation x2, loops' own time, local(): lax.linalg.tridiagonal_solve(lower_diag, main_diag, upper_diag, jnp.eye(s...  180 us
    div x6, other arithmetic, settle(): (suf_first - suf_tips[0] * (own_last - own_tips[2] * lower_value)) / (1.0...  80.8 us
    div x5, other arithmetic, local(): lax.linalg.tridiagonal_solve(lower_diag, main_diag, upper_diag, jnp.eye(s...  80.3 us
    add x6, other arithmetic, right_side(): return state_field + spread - transport + mixing  62.1 us
    sub x3, other arithmetic, local(): lax.linalg.tridiagonal_solve(lower_diag, main_diag, upper_diag, jnp.eye(s...  60.5 us
    unnamed x60, local copies, waits for them, and re-layouts  53.3 us
    all_gather x6, blocking collectives, interface(): lax.all_gather(first_row[None], 'rad', axis=0, tiled=True)  45.4 us
    ppermute x18, starting transfers between devices, padded(): lax.ppermute(lax.slice_in_dim(block, block.shape[dim] - width, None, axis...  43.1 us
  transfers between devices with their start and end apart: 36, of which 0 were waited for; matrix products, arithmetic and copies ran while one was open for 33% of the time, Pallas kernels for 0%

commit v1 on v0

--- a/solution.py
+++ b/solution.py
@@ -9,6 +9,13 @@
 theta_rate = 0.25
 axial_mixing = 0.25
 azimuth_mixing = 0.25
+
+
+def swapped_in(x, mesh_axis, d):
+    n_dev = lax.axis_size(mesh_axis)
+    tiles = jnp.stack([x for _ in range(n_dev)])
+    tiles = lax.all_to_all(tiles, mesh_axis, split_axis=0, concat_axis=0)
+    return jnp.concatenate(tiles, axis=d)
 
 
 def padded(block, sides, width, periodic):
@@ -155,7 +162,7 @@
     )
     every_first, every_last = (
         lax.all_gather(first_row[None], "rad", axis=0, tiled=True),
-        lax.all_gather(last_row[None], "rad", axis=0, tiled=True),
+        swapped_in(last_row[None], "rad", 0),
     )
     position = lax.axis_index("rad")
     slab_count = lax.axis_size("rad")

time: 998 us -> 992 us (level)
  blocking collectives: 84.3 us -> 38.4 us
  starting transfers between devices: 81.3 us -> 115 us
    all_to_all x0 -> x6, starting transfers between devices: none -> 34.2 us  [swapped_in(): tiles = lax.all_to_all(tiles, mesh_axis, split_axis=0, concat_axis=0)]
    all_gather x6 -> x0, blocking collectives: 32.9 us -> none  [interface(): lax.all_gather(last_row[None], 'rad', axis=0, tiled=True)]
    all_gather x6, blocking collectives: 45.4 us -> 32.4 us  [interface(): lax.all_gather(first_row[None], 'rad', axis=0, tiled=True)]
  transfers between devices with their start and end apart: 36 -> 42, of which waited for: 0 -> 0; matrix products, arithmetic and copies ran while one was open for 33% -> 33% of each run, Pallas kernels for 0% -> 0%
where the time goes in v1:
time: 992 us; the launch traced here: 974 us
  other arithmetic  334 us (34%)
  loops' own time  179 us (18%)
  local copies, waits for them, and re-layouts  169 us (17%)
  between operations  126 us (13%)
  starting transfers between devices  115 us (12%)
  blocking collectives  38.4 us (4%)
  matrix products  11.6 us (1%)
    another operation x2, loops' own time, local(): lax.linalg.tridiagonal_solve(lower_diag, main_diag, upper_diag, jnp.eye(s...  179 us
    div x6, other arithmetic, settle(): (suf_first - suf_tips[0] * (own_last - own_tips[2] * lower_value)) / (1.0...  81.8 us
    div x5, other arithmetic, local(): lax.linalg.tridiagonal_solve(lower_diag, main_diag, upper_diag, jnp.eye(s...  79.8 us
    add x6, other arithmetic, right_side(): return state_field + spread - transport + mixing  62.8 us
    sub x3, other arithmetic, local(): lax.linalg.tridiagonal_solve(lower_diag, main_diag, upper_diag, jnp.eye(s...  61.3 us
    unnamed x60, local copies, waits for them, and re-layouts  53.2 us
    ppermute x18, starting transfers between devices, padded(): lax.ppermute(lax.slice_in_dim(block, block.shape[dim] - width, None, axis...  43.1 us
    broadcast_in_dim x17, other arithmetic, local(): lax.linalg.tridiagonal_solve(lower_diag, main_diag, upper_diag, jnp.eye(s...  42.5 us
  transfers between devices with their start and end apart: 42, of which 0 were waited for; matrix products, arithmetic and copies ran while one was open for 33% of the time, Pallas kernels for 0%

profile of v1, /device:TPU:0, one launch (start us, length us, event | category | flops | bytes accessed | tf_op | source)
XLA Modules:
  0.0 974.4 jit_solution(9999021812344193716)
XLA Ops:
  16.5 5.7 collective-permute-start.3
  26.1 252.6 %while.32 = (s32[]{:T(128)}, f32[]{:T(128)}, f32[128]{0:T(128)S(1)}, f32[3,32]{1,0:T(4,128)S(1)}, f32[3,32,128]{2,1,0:T(8,128)S(1)}, /*index=5*/f32[3,32]{1,0:T(...) while((s32[]{:T(128)}, f32[]{:T(128)}, ...), condition=%wide.region_1.2_spmd, body=%wide.region_0.1_spmd.sunk | while | flops 12417 | bytes 104185 | solution.py:191
  90.1 19.9 %fusion.565 = (f32[128]{0:T(128)S(1)}, f32[128]{0:T(128)S(1)}, f32[128]{0:T(128)S(1)}, f32[128]{0:T(128)S(1)}, f32[128]{0:T(128)S(1)}, /*index=5*/f32[128]{0:T(1...) fusion(f32[3,32,128]{2,1,0:T(8,128)S(1)} %get-tuple-element.125, ...), kind=kLoop, calls=%fused_computation.41.clone.1 | loop fusion | flops 12288 | bytes 33664 | tf_op jit(solution)/shard_map/while/body/eval_jaxpr/div | solution.py:191
  174.3 19.9 %fusion.565 = (f32[128]{0:T(128)S(1)}, f32[128]{0:T(128)S(1)}, f32[128]{0:T(128)S(1)}, f32[128]{0:T(128)S(1)}, f32[128]{0:T(128)S(1)}, /*index=5*/f32[128]{0:T(1...) fusion(f32[3,32,128]{2,1,0:T(8,128)S(1)} %get-tuple-element.125, ...), kind=kLoop, calls=%fused_computation.41.clone.1 | loop fusion | flops 12288 | bytes 33664 | tf_op jit(solution)/shard_map/while/body/eval_jaxpr/div | solution.py:191
  258.5 19.9 %fusion.565 = (f32[128]{0:T(128)S(1)}, f32[128]{0:T(128)S(1)}, f32[128]{0:T(128)S(1)}, f32[128]{0:T(128)S(1)}, f32[128]{0:T(128)S(1)}, /*index=5*/f32[128]{0:T(1...) fusion(f32[3,32,128]{2,1,0:T(8,128)S(1)} %get-tuple-element.125, ...), kind=kLoop, calls=%fused_computation.41.clone.1 | loop fusion | flops 12288 | bytes 33664 | tf_op jit(solution)/shard_map/while/body/eval_jaxpr/div | solution.py:191
  341.0 19.5 %fusion.330 = (f32[128]{0:T(128)S(1)}, f32[128]{0:T(128)S(1)}, f32[128]{0:T(128)S(1)}, f32[128]{0:T(128)S(1)}, f32[128]{0:T(128)S(1)}, /*index=5*/f32[128]{0:T(1...) fusion(f32[128,128]{1,0:T(8,128)S(1)} %fusion.256, ...), kind=kLoop, calls=%fused_computation.656 | loop fusion | flops 11904 | bytes 32504 | tf_op jit(solution)/shard_map/eval_jaxpr/div | solution.py:191
  360.9 66.0 %while.33 = (s32[]{:T(128)}, f32[128]{0:T(128)S(1)}, f32[3,32,128]{2,1,0:T(8,128)S(1)}, f32[3,32,128]{2,1,0:T(8,128)S(1)}, f32[3,32]{1,0:T(4,128)S(1)}, /*index=...) while((s32[]{:T(128)}, f32[128]{0:T(128)S(1)}, ...), condition=%wide.region_3.4_spmd, body=%wide.region_2.3_spmd.sunk | while | flops 8226 | bytes 101341 | solution.py:191
  362.3 20.4 %fusion.568 = (f32[128]{0:T(128)S(1)}, f32[128]{0:T(128)S(1)}, f32[128]{0:T(128)S(1)}, f32[128]{0:T(128)S(1)}, f32[128]{0:T(128)S(1)}, /*index=5*/f32[128]{0:T(1...) fusion(f32[3,32,128]{2,1,0:T(8,128)S(1)} %get-tuple-element.136, ...), kind=kLoop, calls=%fused_computation.169.clone.1 | loop fusion | flops 8192 | bytes 33536 | tf_op jit(solution)/shard_map/while/body/eval_jaxpr/sub | solution.py:191
  384.3 20.4 %fusion.568 = (f32[128]{0:T(128)S(1)}, f32[128]{0:T(128)S(1)}, f32[128]{0:T(128)S(1)}, f32[128]{0:T(128)S(1)}, f32[128]{0:T(128)S(1)}, /*index=5*/f32[128]{0:T(1...) fusion(f32[3,32,128]{2,1,0:T(8,128)S(1)} %get-tuple-element.136, ...), kind=kLoop, calls=%fused_computation.169.clone.1 | loop fusion | flops 8192 | bytes 33536 | tf_op jit(solution)/shard_map/while/body/eval_jaxpr/sub | solution.py:191
  406.4 20.4 %fusion.568 = (f32[128]{0:T(128)S(1)}, f32[128]{0:T(128)S(1)}, f32[128]{0:T(128)S(1)}, f32[128]{0:T(128)S(1)}, f32[128]{0:T(128)S(1)}, /*index=5*/f32[128]{0:T(1...) fusion(f32[3,32,128]{2,1,0:T(8,128)S(1)} %get-tuple-element.136, ...), kind=kLoop, calls=%fused_computation.169.clone.1 | loop fusion | flops 8192 | bytes 33536 | tf_op jit(solution)/shard_map/while/body/eval_jaxpr/sub | solution.py:191
  436.2 3.2 fusion.375
  442.4 3.2 fusion.373
  445.6 3.1 fusion.372
  493.8 6.0 all-reduce
  576.0 15.8 %fusion.181 = f32[128,16,256]{2,1,0:T(8,128)S(1)} fusion(bf16[128,16,256]{2,1,0:T(8,128)(2,1)S(1)} %copy-done, bf16[128,16,256]{2,1,0:T(8,128)(2,1)S(1)} %copy-done.1, f32[128,16,256]{2,1,0:T(8,128)} %param.14, f32[1,16,256]{2,1,0:T(8,128)} %collective-permute-done.1, f32[1,16,256]{2,1,0:T(8,128)S(1)} %collective-permute-done, ...), kind=kLoop, calls=%fused_computation.299 | loop fusion | flops 28311552 | bytes 10816000 | tf_op jit(solution)/shard_map/add | solution.py:93
  596.1 3.6 all-to-all-start
  603.6 5.6 all-gather.1
  609.2 13.6 %subtract_divide_fusion.5 = (f32[1,4096]{1,0:T(1,128)S(1)}, f32[1,4096]{1,0:T(1,128)S(1)}) fusion(f32[]{:T(128)} %bitcast.672, f32[]{:T(128)S(6)} %sub.2797, f32[]{:T(128)S(1)} %bitcast.2392, f32[128,4096]{1,0:T(8,128)S(1)} %fusion.531, f32[]{:T(128)S(6)} %sub.2802, f32[]{:T(128)} %bitcast.670, f32[]{:T(128)} %bitcast.640, f32[]{:T(128)} %bitcast.639, ...), kind=kLoop, calls=%fused_computation.547 | loop fusion | flops 286720 | bytes 196748 | tf_op jit(solution)/shard_map/div | solution.py:150
  627.2 3.8 collective-permute-start.10
  638.2 5.1 collective-permute-start.9
  653.7 9.4 fusion.185
  667.4 5.9 all-to-all-start.1
  673.4 5.3 all-gather.2
  678.7 13.6 %subtract_divide_fusion.4 = (f32[1,4096]{1,0:T(1,128)S(1)}, f32[1,4096]{1,0:T(1,128)S(1)}) fusion(f32[]{:T(128)} %bitcast.672, f32[]{:T(128)S(6)} %sub.2797, f32[]{:T(128)S(1)} %bitcast.2393, f32[128,4096]{1,0:T(8,128)S(1)} %fusion.532, f32[]{:T(128)S(6)} %sub.2802, f32[]{:T(128)} %bitcast.670, f32[]{:T(128)} %bitcast.640, f32[]{:T(128)} %bitcast.639, ...), kind=kLoop, calls=%fused_computation.546 | loop fusion | flops 286720 | bytes 196748 | tf_op jit(solution)/shard_map/div | solution.py:150
  696.7 3.8 collective-permute-start.16
  707.8 5.1 collective-permute-start.15
  723.3 9.4 fusion.189
  737.0 6.2 all-to-all-start.2
  743.2 5.3 all-gather.3
  748.5 13.6 %subtract_divide_fusion.3 = (f32[1,4096]{1,0:T(1,128)S(1)}, f32[1,4096]{1,0:T(1,128)S(1)}) fusion(f32[]{:T(128)} %bitcast.672, f32[]{:T(128)S(6)} %sub.2797, f32[]{:T(128)S(1)} %bitcast.2394, f32[128,4096]{1,0:T(8,128)S(1)} %fusion.533, f32[]{:T(128)S(6)} %sub.2802, f32[]{:T(128)} %bitcast.670, f32[]{:T(128)} %bitcast.640, f32[]{:T(128)} %bitcast.639, ...), kind=kLoop, calls=%fused_computation.545 | loop fusion | flops 286720 | bytes 196748 | tf_op jit(solution)/shard_map/div | solution.py:150
  766.5 3.8 collective-permute-start.22
  777.6 5.1 collective-permute-start.21
  793.4 9.4 fusion.193
  807.0 6.2 all-to-all-start.3
  813.2 5.3 all-gather.4
  818.6 13.6 %subtract_divide_fusion.2 = (f32[1,4096]{1,0:T(1,128)S(1)}, f32[1,4096]{1,0:T(1,128)S(1)}) fusion(f32[]{:T(128)} %bitcast.672, f32[]{:T(128)S(6)} %sub.2797, f32[]{:T(128)S(1)} %bitcast.2395, f32[128,4096]{1,0:T(8,128)S(1)} %fusion.534, f32[]{:T(128)S(6)} %sub.2802, f32[]{:T(128)} %bitcast.670, f32[]{:T(128)} %bitcast.640, f32[]{:T(128)} %bitcast.639, ...), kind=kLoop, calls=%fused_computation.544 | loop fusion | flops 286720 | bytes 196748 | tf_op jit(solution)/shard_map/div | solution.py:150
  836.5 3.8 collective-permute-start.28
  847.6 5.1 collective-permute-start.27
  863.1 9.4 fusion.197
  876.8 6.2 all-to-all-start.4
  883.0 5.3 all-gather.5
  888.3 13.6 %subtract_divide_fusion.1 = (f32[1,4096]{1,0:T(1,128)S(1)}, f32[1,4096]{1,0:T(1,128)S(1)}) fusion(f32[]{:T(128)} %bitcast.672, f32[]{:T(128)S(6)} %sub.2797, f32[]{:T(128)S(1)} %bitcast.2396, f32[128,4096]{1,0:T(8,128)S(1)} %fusion.535, f32[]{:T(128)S(6)} %sub.2802, f32[]{:T(128)} %bitcast.670, f32[]{:T(128)} %bitcast.640, f32[]{:T(128)} %bitcast.639, ...), kind=kLoop, calls=%fused_computation.543 | loop fusion | flops 286720 | bytes 196748 | tf_op jit(solution)/shard_map/div | solution.py:150
  906.3 3.8 collective-permute-start.34
  917.4 5.1 collective-permute-start.33
  932.9 9.4 fusion.201
  946.6 6.2 all-to-all-start.5
  952.8 5.3 all-gather.6
  958.1 13.6 %subtract_divide_fusion = (f32[1,4096]{1,0:T(1,128)S(1)}, f32[1,4096]{1,0:T(1,128)S(1)}) fusion(f32[]{:T(128)} %bitcast.672, f32[]{:T(128)S(6)} %sub.2797, f32[]{:T(128)S(1)} %bitcast.2397, f32[128,4096]{1,0:T(8,128)S(1)} %fusion.536, f32[]{:T(128)S(6)} %sub.2802, f32[]{:T(128)} %bitcast.670, f32[]{:T(128)} %bitcast.640, f32[]{:T(128)} %bitcast.639, ...), kind=kLoop, calls=%fused_computation.542 | loop fusion | flops 286720 | bytes 196748 | tf_op jit(solution)/shard_map/div | solution.py:150
  (345 shorter events, 251.6 us)
Async XLA Ops:
  1.4 574.6 %collective-permute-start.1 = (f32[1,16,256]{2,1,0:T(8,128)}, f32[1,16,256]{2,1,0:T(8,128)}, u32[]{:S(2)}, u32[]{:S(2)}) collective-permute-start(f32[1,16,256]{2,1,0:T(8,128)} %get-tuple-element.511), channel_id=1, source_target_pairs={{0,1},{1,2},{2,3},{4,5},{5,6},{6,7},{8,9},{9,10},{10,11},{12,13},{... | collective-permute-start | bytes 49160 | tf_op jit(solution)/shard_map/ppermute | solution.py:28
  6.8 569.1 %collective-permute-start.5 = (f32[128,2,256]{2,1,0:T(2,128)}, f32[128,2,256]{2,1,0:T(2,128)S(1)}, u32[]{:S(2)}, u32[]{:S(2)}) collective-permute-start(f32[128,2,256]{2,1,0:T(2,128)} %get-tuple-element.509), channel_id=1, source_target_pairs={{0,4},{4,8},{8,12},{12,0},{1,5},{5,9},{9,13},{13,1},{2,6},{6,10},{... | collective-permute-start | bytes 786440 | tf_op jit(solution)/shard_map/ppermute | solution.py:28
  9.2 565.0 %collective-permute-start.4 = (f32[128,2,256]{2,1,0:T(2,128)}, f32[128,2,256]{2,1,0:T(2,128)}, u32[]{:S(2)}, u32[]{:S(2)}) collective-permute-start(f32[128,2,256]{2,1,0:T(2,128)} %get-tuple-element.508), channel_id=1, source_target_pairs={{4,0},{8,4},{12,8},{0,12},{5,1},{9,5},{13,9},{1,13},{6,2},{10,6},{... | collective-permute-start | bytes 786440 | tf_op jit(solution)/shard_map/ppermute | solution.py:31
  13.1 9.1 copy-start.10
  14.2 554.8 %collective-permute-start.2 = (f32[128,16,2]{0,1,2:T(8,128)}, f32[128,16,2]{0,1,2:T(8,128)}, u32[]{:S(2)}, u32[]{:S(2)}) collective-permute-start(f32[128,16,2]{0,1,2:T(8,128)} %copy.101), channel_id=1, source_target_pairs={{16,0},{17,1},{18,2},{19,3},{20,4},{21,5},{22,6},{23,7},{24,8},{25... | collective-permute-start | bytes 49160 | tf_op jit(solution)/shard_map/ppermute | solution.py:31
  16.5 555.5 %collective-permute-start.3 = (f32[128,16,2]{0,1,2:T(8,128)}, f32[128,16,2]{0,1,2:T(8,128)}, u32[]{:S(2)}, u32[]{:S(2)}) collective-permute-start(f32[128,16,2]{0,1,2:T(8,128)} %copy.102), channel_id=1, source_target_pairs={{0,16},{1,17},{2,18},{3,19},{4,20},{5,21},{6,22},{7,23},{8,24},{9,... | collective-permute-start | bytes 49160 | tf_op jit(solution)/shard_map/ppermute | solution.py:28
  278.7 148.2 %copy-start.8 = (f32[3,32,128]{2,1,0:T(8,128)}, f32[3,32,128]{2,1,0:T(8,128)S(1)}, u32[]{:S(2)}) copy-start(f32[3,32,128]{2,1,0:T(8,128)S(1)} %get-tuple-element.159) | copy-start | bytes 147460
  470.9 87.8 %copy-start.2 = (f32[128,16,256]{2,1,0:T(8,128)S(1)}, f32[128,16,256]{2,1,0:T(8,128)}, u32[]{:S(2)}) copy-start(f32[128,16,256]{2,1,0:T(8,128)} %param.14) | copy-start | bytes 6291460
  558.6 10.4 %copy-start.9 = (f32[1,16,256]{2,1,0:T(8,128)S(1)}, f32[1,16,256]{2,1,0:T(8,128)}, u32[]{:S(2)}) copy-start(f32[1,16,256]{2,1,0:T(8,128)} %get-tuple-element.510) | copy-start | bytes 49156
  560.2 15.8 %copy-start = (bf16[128,16,256]{2,1,0:T(8,128)(2,1)S(1)}, bf16[128,16,256]{2,1,0:T(8,128)(2,1)}, u32[]{:S(2)}) copy-start(bf16[128,16,256]{2,1,0:T(8,128)(2,1)} %param.15) | copy-start | bytes 3145732
  560.2 15.8 %copy-start.1 = (bf16[128,16,256]{2,1,0:T(8,128)(2,1)S(1)}, bf16[128,16,256]{2,1,0:T(8,128)(2,1)}, u32[]{:S(2)}) copy-start(bf16[128,16,256]{2,1,0:T(8,128)(2,1)} %param.16) | copy-start | bytes 3145732
  569.0 6.9 collective-permute-start
  596.1 13.1 %all-to-all-start = ((f32[4,1,4096]{2,1,0:T(1,128)}), f32[4,1,4096]{2,1,0:T(1,128)S(1)}, u32[]{:S(2)}, u32[]{:S(2)}) async-start(f32[4,1,4096]{2,1,0:T(1,128)} %stack.741), calls=%async_computation | async-start | bytes 131072 | tf_op jit(solution)/shard_map/all_to_all | solution.py:17
  627.2 26.6 %collective-permute-start.11 = (f32[128,2,256]{2,1,0:T(2,128)}, f32[128,2,256]{2,1,0:T(2,128)S(1)}, u32[]{:S(2)}, u32[]{:S(2)}) collective-permute-start(f32[128,2,256]{2,1,0:T(2,128)} %get-tuple-element.503), channel_id=1, source_target_pairs={{0,4},{4,8},{8,12},{12,0},{1,5},{5,9},{9,13},{13,1},{2,6},{6,10},{... | collective-permute-start | bytes 786440 | tf_op jit(solution)/shard_map/ppermute | solution.py:28
  627.2 24.8 %collective-permute-start.10 = (f32[128,2,256]{2,1,0:T(2,128)}, f32[128,2,256]{2,1,0:T(2,128)}, u32[]{:S(2)}, u32[]{:S(2)}) collective-permute-start(f32[128,2,256]{2,1,0:T(2,128)} %get-tuple-element.502), channel_id=1, source_target_pairs={{4,0},{8,4},{12,8},{0,12},{5,1},{9,5},{13,9},{1,13},{6,2},{10,6},{... | collective-permute-start | bytes 786440 | tf_op jit(solution)/shard_map/ppermute | solution.py:31
  634.7 12.2 %collective-permute-start.8 = (f32[128,16,2]{0,1,2:T(8,128)}, f32[128,16,2]{0,1,2:T(8,128)S(1)}, u32[]{:S(2)}, u32[]{:S(2)}) collective-permute-start(f32[128,16,2]{0,1,2:T(8,128)} %copy.103), channel_id=1, source_target_pairs={{16,0},{17,1},{18,2},{19,3},{20,4},{21,5},{22,6},{23,7},{24,8},{25... | collective-permute-start | bytes 49160 | tf_op jit(solution)/shard_map/ppermute | solution.py:31
  638.2 11.6 %collective-permute-start.9 = (f32[128,16,2]{0,1,2:T(8,128)}, f32[128,16,2]{0,1,2:T(8,128)}, u32[]{:S(2)}, u32[]{:S(2)}) collective-permute-start(f32[128,16,2]{0,1,2:T(8,128)} %copy.104), channel_id=1, source_target_pairs={{0,16},{1,17},{2,18},{3,19},{4,20},{5,21},{6,22},{7,23},{8,24},{9,... | collective-permute-start | bytes 49160 | tf_op jit(solution)/shard_map/ppermute | solution.py:28
  645.0 8.7 collective-permute-start.7
  646.9 6.8 collective-permute-start.6
  667.4 11.3 %all-to-all-start.1 = ((f32[4,1,4096]{2,1,0:T(1,128)}), f32[4,1,4096]{2,1,0:T(1,128)S(1)}, u32[]{:S(2)}, u32[]{:S(2)}) async-start(f32[4,1,4096]{2,1,0:T(1,128)} %stack.783), calls=%async_computation.1 | async-start | bytes 131072 | tf_op jit(solution)/shard_map/all_to_all | solution.py:17
  696.7 26.6 %collective-permute-start.17 = (f32[128,2,256]{2,1,0:T(2,128)}, f32[128,2,256]{2,1,0:T(2,128)S(1)}, u32[]{:S(2)}, u32[]{:S(2)}) collective-permute-start(f32[128,2,256]{2,1,0:T(2,128)} %get-tuple-element.497), channel_id=1, source_target_pairs={{0,4},{4,8},{8,12},{12,0},{1,5},{5,9},{9,13},{13,1},{2,6},{6,10},{... | collective-permute-start | bytes 786440 | tf_op jit(solution)/shard_map/ppermute | solution.py:28
  696.7 24.8 %collective-permute-start.16 = (f32[128,2,256]{2,1,0:T(2,128)}, f32[128,2,256]{2,1,0:T(2,128)}, u32[]{:S(2)}, u32[]{:S(2)}) collective-permute-start(f32[128,2,256]{2,1,0:T(2,128)} %get-tuple-element.496), channel_id=1, source_target_pairs={{4,0},{8,4},{12,8},{0,12},{5,1},{9,5},{13,9},{1,13},{6,2},{10,6},{... | collective-permute-start | bytes 786440 | tf_op jit(solution)/shard_map/ppermute | solution.py:31
  704.3 12.2 %collective-permute-start.14 = (f32[128,16,2]{0,1,2:T(8,128)}, f32[128,16,2]{0,1,2:T(8,128)S(1)}, u32[]{:S(2)}, u32[]{:S(2)}) collective-permute-start(f32[128,16,2]{0,1,2:T(8,128)} %copy.105), channel_id=1, source_target_pairs={{16,0},{17,1},{18,2},{19,3},{20,4},{21,5},{22,6},{23,7},{24,8},{25... | collective-permute-start | bytes 49160 | tf_op jit(solution)/shard_map/ppermute | solution.py:31
  707.8 11.6 %collective-permute-start.15 = (f32[128,16,2]{0,1,2:T(8,128)}, f32[128,16,2]{0,1,2:T(8,128)}, u32[]{:S(2)}, u32[]{:S(2)}) collective-permute-start(f32[128,16,2]{0,1,2:T(8,128)} %copy.106), channel_id=1, source_target_pairs={{0,16},{1,17},{2,18},{3,19},{4,20},{5,21},{6,22},{7,23},{8,24},{9,... | collective-permute-start | bytes 49160 | tf_op jit(solution)/shard_map/ppermute | solution.py:28
  714.6 8.7 collective-permute-start.13
  716.5 6.9 collective-permute-start.12
  737.0 11.5 %all-to-all-start.2 = ((f32[4,1,4096]{2,1,0:T(1,128)}), f32[4,1,4096]{2,1,0:T(1,128)S(1)}, u32[]{:S(2)}, u32[]{:S(2)}) async-start(f32[4,1,4096]{2,1,0:T(1,128)} %stack.824), calls=%async_computation.2 | async-start | bytes 131072 | tf_op jit(solution)/shard_map/all_to_all | solution.py:17
  766.5 26.8 %collective-permute-start.23 = (f32[128,2,256]{2,1,0:T(2,128)}, f32[128,2,256]{2,1,0:T(2,128)S(1)}, u32[]{:S(2)}, u32[]{:S(2)}) collective-permute-start(f32[128,2,256]{2,1,0:T(2,128)} %get-tuple-element.491), channel_id=1, source_target_pairs={{0,4},{4,8},{8,12},{12,0},{1,5},{5,9},{9,13},{13,1},{2,6},{6,10},{... | collective-permute-start | bytes 786440 | tf_op jit(solution)/shard_map/ppermute | solution.py:28
  766.5 25.0 %collective-permute-start.22 = (f32[128,2,256]{2,1,0:T(2,128)}, f32[128,2,256]{2,1,0:T(2,128)}, u32[]{:S(2)}, u32[]{:S(2)}) collective-permute-start(f32[128,2,256]{2,1,0:T(2,128)} %get-tuple-element.490), channel_id=1, source_target_pairs={{4,0},{8,4},{12,8},{0,12},{5,1},{9,5},{13,9},{1,13},{6,2},{10,6},{... | collective-permute-start | bytes 786440 | tf_op jit(solution)/shard_map/ppermute | solution.py:31
  774.1 12.2 %collective-permute-start.20 = (f32[128,16,2]{0,1,2:T(8,128)}, f32[128,16,2]{0,1,2:T(8,128)S(1)}, u32[]{:S(2)}, u32[]{:S(2)}) collective-permute-start(f32[128,16,2]{0,1,2:T(8,128)} %copy.107), channel_id=1, source_target_pairs={{16,0},{17,1},{18,2},{19,3},{20,4},{21,5},{22,6},{23,7},{24,8},{25... | collective-permute-start | bytes 49160 | tf_op jit(solution)/shard_map/ppermute | solution.py:31
  777.6 11.8 %collective-permute-start.21 = (f32[128,16,2]{0,1,2:T(8,128)}, f32[128,16,2]{0,1,2:T(8,128)}, u32[]{:S(2)}, u32[]{:S(2)}) collective-permute-start(f32[128,16,2]{0,1,2:T(8,128)} %copy.108), channel_id=1, source_target_pairs={{0,16},{1,17},{2,18},{3,19},{4,20},{5,21},{6,22},{7,23},{8,24},{9,... | collective-permute-start | bytes 49160 | tf_op jit(solution)/shard_map/ppermute | solution.py:28
  784.4 8.9 collective-permute-start.19
  786.3 7.0 collective-permute-start.18
  807.0 11.5 %all-to-all-start.3 = ((f32[4,1,4096]{2,1,0:T(1,128)}), f32[4,1,4096]{2,1,0:T(1,128)S(1)}, u32[]{:S(2)}, u32[]{:S(2)}) async-start(f32[4,1,4096]{2,1,0:T(1,128)} %stack.865), calls=%async_computation.3 | async-start | bytes 131072 | tf_op jit(solution)/shard_map/all_to_all | solution.py:17
  836.5 26.6 %collective-permute-start.29 = (f32[128,2,256]{2,1,0:T(2,128)}, f32[128,2,256]{2,1,0:T(2,128)S(1)}, u32[]{:S(2)}, u32[]{:S(2)}) collective-permute-start(f32[128,2,256]{2,1,0:T(2,128)} %get-tuple-element.485), channel_id=1, source_target_pairs={{0,4},{4,8},{8,12},{12,0},{1,5},{5,9},{9,13},{13,1},{2,6},{6,10},{... | collective-permute-start | bytes 786440 | tf_op jit(solution)/shard_map/ppermute | solution.py:28
  836.5 24.8 %collective-permute-start.28 = (f32[128,2,256]{2,1,0:T(2,128)}, f32[128,2,256]{2,1,0:T(2,128)}, u32[]{:S(2)}, u32[]{:S(2)}) collective-permute-start(f32[128,2,256]{2,1,0:T(2,128)} %get-tuple-element.484), channel_id=1, source_target_pairs={{4,0},{8,4},{12,8},{0,12},{5,1},{9,5},{13,9},{1,13},{6,2},{10,6},{... | collective-permute-start | bytes 786440 | tf_op jit(solution)/shard_map/ppermute | solution.py:31
  844.1 12.2 %collective-permute-start.26 = (f32[128,16,2]{0,1,2:T(8,128)}, f32[128,16,2]{0,1,2:T(8,128)S(1)}, u32[]{:S(2)}, u32[]{:S(2)}) collective-permute-start(f32[128,16,2]{0,1,2:T(8,128)} %copy.109), channel_id=1, source_target_pairs={{16,0},{17,1},{18,2},{19,3},{20,4},{21,5},{22,6},{23,7},{24,8},{25... | collective-permute-start | bytes 49160 | tf_op jit(solution)/shard_map/ppermute | solution.py:31
  847.6 11.6 %collective-permute-start.27 = (f32[128,16,2]{0,1,2:T(8,128)}, f32[128,16,2]{0,1,2:T(8,128)}, u32[]{:S(2)}, u32[]{:S(2)}) collective-permute-start(f32[128,16,2]{0,1,2:T(8,128)} %copy.110), channel_id=1, source_target_pairs={{0,16},{1,17},{2,18},{3,19},{4,20},{5,21},{6,22},{7,23},{8,24},{9,... | collective-permute-start | bytes 49160 | tf_op jit(solution)/shard_map/ppermute | solution.py:28
  854.4 8.7 collective-permute-start.25
  856.3 6.8 collective-permute-start.24
  876.8 11.5 %all-to-all-start.4 = ((f32[4,1,4096]{2,1,0:T(1,128)}), f32[4,1,4096]{2,1,0:T(1,128)S(1)}, u32[]{:S(2)}, u32[]{:S(2)}) async-start(f32[4,1,4096]{2,1,0:T(1,128)} %stack.906), calls=%async_computation.4 | async-start | bytes 131072 | tf_op jit(solution)/shard_map/all_to_all | solution.py:17
  906.3 26.6 %collective-permute-start.35 = (f32[128,2,256]{2,1,0:T(2,128)}, f32[128,2,256]{2,1,0:T(2,128)S(1)}, u32[]{:S(2)}, u32[]{:S(2)}) collective-permute-start(f32[128,2,256]{2,1,0:T(2,128)} %get-tuple-element.479), channel_id=1, source_target_pairs={{0,4},{4,8},{8,12},{12,0},{1,5},{5,9},{9,13},{13,1},{2,6},{6,10},{... | collective-permute-start | bytes 786440 | tf_op jit(solution)/shard_map/ppermute | solution.py:28
  906.3 24.8 %collective-permute-start.34 = (f32[128,2,256]{2,1,0:T(2,128)}, f32[128,2,256]{2,1,0:T(2,128)}, u32[]{:S(2)}, u32[]{:S(2)}) collective-permute-start(f32[128,2,256]{2,1,0:T(2,128)} %get-tuple-element.478), channel_id=1, source_target_pairs={{4,0},{8,4},{12,8},{0,12},{5,1},{9,5},{13,9},{1,13},{6,2},{10,6},{... | collective-permute-start | bytes 786440 | tf_op jit(solution)/shard_map/ppermute | solution.py:31
  913.9 12.2 %collective-permute-start.32 = (f32[128,16,2]{0,1,2:T(8,128)}, f32[128,16,2]{0,1,2:T(8,128)S(1)}, u32[]{:S(2)}, u32[]{:S(2)}) collective-permute-start(f32[128,16,2]{0,1,2:T(8,128)} %copy.111), channel_id=1, source_target_pairs={{16,0},{17,1},{18,2},{19,3},{20,4},{21,5},{22,6},{23,7},{24,8},{25... | collective-permute-start | bytes 49160 | tf_op jit(solution)/shard_map/ppermute | solution.py:31
  917.4 11.6 %collective-permute-start.33 = (f32[128,16,2]{0,1,2:T(8,128)}, f32[128,16,2]{0,1,2:T(8,128)}, u32[]{:S(2)}, u32[]{:S(2)}) collective-permute-start(f32[128,16,2]{0,1,2:T(8,128)} %copy.112), channel_id=1, source_target_pairs={{0,16},{1,17},{2,18},{3,19},{4,20},{5,21},{6,22},{7,23},{8,24},{9,... | collective-permute-start | bytes 49160 | tf_op jit(solution)/shard_map/ppermute | solution.py:28
  924.2 8.7 collective-permute-start.31
  926.1 6.9 collective-permute-start.30
  946.6 11.5 %all-to-all-start.5 = ((f32[4,1,4096]{2,1,0:T(1,128)}), f32[4,1,4096]{2,1,0:T(1,128)S(1)}, u32[]{:S(2)}, u32[]{:S(2)}) async-start(f32[4,1,4096]{2,1,0:T(1,128)} %stack.947), calls=%async_computation.5 | async-start | bytes 131072 | tf_op jit(solution)/shard_map/all_to_all | solution.py:17
  (5 other events, 6.6 us)
